TPU v7x, 32 devices: a whole 2x2x4 slice. The times are simulated.
32 devices in a mesh: dp: 8 (over z, x), mp: 4 (over y, core).
Axes of the slice: x: 2, y: 2, z: 4, core: 2. Of those that a mesh axis runs over, the one named last changes fastest.
Arguments:
- tokens: bfloat16 [8192, 8192], P(('dp', 'mp')), may hold values from -6 to 6
- key_value_weight: bfloat16 [8192, 2048], P(None, 'mp'), may hold values from -0.0625 to 0.0625
- adapter_down_weight: bfloat16 [16, 8192, 128], P(None, ('dp', 'mp')), may hold values from -0.0625 to 0.0625
- adapter_up_weight: bfloat16 [16, 64, 2048], P(None, 'dp', 'mp'), may hold values from -1 to 1
- adapter_per_request: int32 [32], replicated, may hold values from 0 to 15
- request_per_segment: int32 [64], replicated, may hold values from 0 to 31, never falling along the last dimension, each value on 1 to 4 neighbouring positions
Outputs:
- kv_out: bfloat16 [8192, 2048], P('dp', 'mp')
Inputs may be any that keep to these rules, and one draw needn't show every extreme that they name: request_per_segment never falls along the segments; every request has 1 to 4 segments, one has exactly 4.
All inputs are finite; a program needn't handle non-finite values.
Results may differ from a plain program's by a relative error of at most 0.0043.
Values may be sent and summed in bfloat16 or wider, within the bound.
A program may use at most 128 MiB of HBM per device.

v0:
```python
import jax
import jax.numpy as jnp
from jax import lax
from jax.sharding import PartitionSpec as P


def on_device(
    tokens,
    key_value_weight,
    adapter_down_weight,
    adapter_up_weight,
    adapter_per_request,
    request_per_segment,
):
    n_dp = lax.axis_size("dp")
    n_mp = lax.axis_size("mp")
    group = lax.axis_index("dp")
    column = lax.axis_index("mp")
    seg_total = request_per_segment.shape[0]
    seg_group = seg_total // n_dp
    seg_adapter = jnp.take(adapter_per_request, request_per_segment, axis=0)
    local_portion = lax.dynamic_slice_in_dim(seg_adapter, group * seg_group, seg_group)
    gathered = lax.all_gather(tokens, "mp", axis=0, tiled=True)
    rows = gathered.shape[0]
    seg_len = rows // seg_group
    width_tile = adapter_down_weight.shape[1]
    double_rank = adapter_down_weight.shape[2]
    rank = double_rank // 2
    column_tile = adapter_up_weight.shape[2]
    base = jnp.dot(gathered, key_value_weight, preferred_element_type=jnp.float32)
    strided = lax.dynamic_index_in_dim(
        gathered.reshape(rows, n_dp, n_mp, width_tile), column, 2, keepdims=False
    ).reshape(seg_group, seg_len, n_dp * width_tile)
    selected_factor = jnp.take(
        lax.all_gather(adapter_down_weight, "dp", axis=1, tiled=True), local_portion, axis=0
    )
    partial_low = jnp.einsum(
        "sti,sir->str", strided, selected_factor, preferred_element_type=jnp.float32
    )
    selected_factor = jnp.take(
        lax.all_gather(adapter_up_weight, "dp", axis=1, tiled=True), local_portion, axis=0
    )
    rank_output = lax.psum(partial_low, "mp").astype(jnp.bfloat16)
    key_width = n_mp * column_tile // 2
    half = column * column_tile // key_width
    low_half = lax.dynamic_slice_in_dim(rank_output, half * rank, rank, 2)
    delta = jnp.einsum(
        "str,src->stc", low_half, selected_factor, preferred_element_type=jnp.float32
    )
    return (base + delta.reshape(rows, column_tile)).astype(jnp.bfloat16)


def solution(mesh):
    placed = (
        P(("dp", "mp"), None),
        P(None, "mp"),
        P(None, ("dp", "mp"), None),
        P(None, "dp", "mp"),
        P(),
        P(),
    )
    return jax.shard_map(
        on_device, mesh=mesh, in_specs=placed, out_specs=P("dp", "mp"), check_vma=False
    )
```

profile of v0, /device:TPU:0, one launch (start us, length us, event | category | flops | bytes accessed | tf_op | source)
XLA Modules:
  0.0 391.5 jit_solution(268744416518577223)
XLA Ops:
  6.5 0.0 copy-start
  6.5 0.0 all-gather.8.cloned.1.call-start
  6.5 0.7 all-gather.8.cloned.1.call-update
  7.3 0.0 all-gather.6.cloned.1.call-start
  7.3 0.7 all-gather.6.cloned.1.call-update
  8.0 0.0 all-gather.4.cloned.1.call-start
  8.1 0.7 all-gather.4.cloned.1.call-update
  8.8 0.0 copy-done.2
  8.8 0.8 gather_fusion
  9.6 0.1 compare_and_fusion
  9.7 42.0 %all-gather.8.cloned.1.call-done = bf16[16,64,512]{2,1,0:T(8,128)(2,1)} async-done(((bf16[16,8,512]{2,1,0:T(8,128)(2,1)}), bf16[16,64,512]{2,1,0:T(8,128)(2,1)}) %all-gather.8.cloned.1.call-update) | async-done | bytes 1048592 | tf_op jit(solution)/shard_map/all_gather | solution.py:41
  51.7 1.8 gather_fusion.2
  53.5 124.2 %all-gather.6.cloned.1.call-done = bf16[16,2048,128]{2,1,0:T(8,128)(2,1)} async-done(((bf16[16,256,128]{2,1,0:T(8,128)(2,1)}), bf16[16,2048,128]{2,1,0:T(8,128)(2,1)}) %all-gather.6.cloned.1.call-update) | async-done | bytes 8388624 | tf_op jit(solution)/shard_map/all_gather | solution.py:35
  177.7 6.5 %gather_fusion.1 = bf16[8,2048,128]{2,1,0:T(8,128)(2,1)} fusion(bf16[16,2048,128]{2,1,0:T(8,128)(2,1)} %all-gather.6.cloned.1.call-done, s32[1024]{0:T(1024)S(1)} %pad_clamp_fusion), kind=kCustom, calls=%fused_computation.1 | custom fusion | bytes 8388640 | tf_op jit(solution)/shard_map/jit(_take)/gather | solution.py:34
  184.2 99.2 %all-gather.4.cloned.1.call-done = bf16[1024,8192]{1,0:T(8,128)(2,1)} async-done(((bf16[256,8192]{1,0:T(8,128)(2,1)}), bf16[1024,8192]{1,0:T(8,128)(2,1)}) %all-gather.4.cloned.1.call-update) | async-done | bytes 16777232 | tf_op jit(solution)/shard_map/all_gather | solution.py:23
  283.4 27.8 %reshape.20 = bf16[1024,8,4,256]{3,2,1,0:T(4,128)(2,1)} reshape(bf16[1024,8192]{1,0:T(8,128)(2,1)} %all-gather.4.cloned.1.call-done) | data formatting | bytes 33554432 | tf_op jit(solution)/shard_map/reshape | solution.py:32
  311.2 29.1 %dynamic-slice_reduce_fusion = bf16[1024,8,256]{2,1,0:T(8,128)(2,1)} fusion(bf16[1024,8,4,256]{3,2,1,0:T(4,128)(2,1)} %reshape.20, s32[]{:T(128)S(6)} %select_n.39), kind=kLoop, calls=%fused_computation.3 | loop fusion | bytes 8388612 | tf_op jit(solution)/shard_map/jit(dynamic_index_in_dim)/dynamic_slice | solution.py:31
  340.3 7.4 %reshape.21 = bf16[8,128,2048]{2,1,0:T(8,128)(2,1)} reshape(bf16[1024,8,256]{2,1,0:T(8,128)(2,1)} %dynamic-slice_reduce_fusion) | data formatting | bytes 8388608 | tf_op jit(solution)/shard_map/reshape | solution.py:33
  347.7 5.0 %fusion = f32[8,128,128]{1,2,0:T(8,128)S(1)} fusion(bf16[8,128,2048]{2,1,0:T(8,128)(2,1)} %reshape.21, bf16[8,2048,128]{2,1,0:T(8,128)(2,1)} %gather_fusion.1, pred[8]{0:T(512)(128)(4,1)S(1)} %get-tuple-element.5), kind=kOutput, calls=%fused_computation.4 | convolution fusion | flops 538968064 | bytes 8912904 | tf_op jit(solution)/shard_map/sti,sir->str/dot_general | solution.py:37
  352.7 16.2 %all-reduce.1 = bf16[8,128,128]{1,2,0:T(8,128)(2,1)S(1)} all-reduce(f32[8,128,128]{1,2,0:T(8,128)S(1)} %fusion), channel_id=1, replica_groups=mesh['dp'=8,'mp'=4] {'mp'}, use_global_device_ids=true, to_apply=%region_0.1 | all-reduce | flops 131072 | bytes 786432 | tf_op jit(solution)/shard_map/psum | solution.py:43
  368.9 0.5 fusion.5
  369.4 0.0 copy-start.1
  369.4 15.6 %fusion.3 = bf16[1024,512]{1,0:T(8,128)(2,1)} fusion(f32[8,128,512]{2,1,0:T(8,128)S(1)} %fusion.5, bf16[1024,8192]{1,0:T(8,128)(2,1)} %all-gather.4.cloned.1.call-done, bf16[8192,512]{1,0:T(8,128)(2,1)} %param.7), kind=kOutput, calls=%fused_computation.8 | convolution fusion | flops 8590983168 | bytes 28311552 | tf_op jit(solution)/shard_map/dot_general | solution.py:30
  385.0 0.0 copy-done.1
  (6 shorter events, 0.0 us)
Async XLA Ops:
  6.5 2.3 copy-start
  6.5 2.2 copy-start.2
  6.5 45.1 %all-gather.8.cloned.1.call-start = ((), (), s32[]{:S(2)}) async-start(), calls=%async_computation.2 | async-start | bytes 1179648 | tf_op jit(solution)/shard_map/all_gather | solution.py:41
  7.3 170.4 %all-gather.6.cloned.1.call-start = ((), (), s32[]{:S(2)}) async-start(), calls=%async_computation.1 | async-start | bytes 9437184 | tf_op jit(solution)/shard_map/all_gather | solution.py:35
  8.0 275.4 %all-gather.4.cloned.1.call-start = ((), (), s32[]{:S(2)}) async-start(), calls=%async_computation | async-start | bytes 20971520 | tf_op jit(solution)/shard_map/all_gather | solution.py:23
  369.4 15.6 %copy-start.1 = (s32[32]{0:T(128)S(1)}, s32[32]{0:T(128)}, u32[]{:S(2)}) copy-start(s32[32]{0:T(128)} %param.10) | copy-start | bytes 388
Sparse Core Ops, SparseCore 0:
  9.4 42.2 all-gather.7
  53.9 123.7 all-gather.5
  179.3 104.1 all-gather.3
where the time goes:
time: 393 us; the launch traced here: 392 us
  waiting for transfers between devices  267 us (68%)
  local copies, waits for them, and re-layouts  73.4 us (19%)
  matrix products  21.1 us (5%)
  blocking collectives  16.2 us (4%)
  between operations  13.2 us (3%)
    all_gather x1, waiting for transfers between devices, on_device(): lax.all_gather(adapter_down_weight, 'dp', axis=1, tiled=True)  124 us
    all_gather x1, waiting for transfers between devices, on_device(): gathered = lax.all_gather(tokens, 'mp', axis=0, tiled=True)  99.2 us
    all_gather x1, waiting for transfers between devices, on_device(): lax.all_gather(adapter_up_weight, 'dp', axis=1, tiled=True)  42 us
    dynamic_slice x1, local copies, waits for them, and re-layouts, on_device(): lax.dynamic_index_in_dim(gathered.reshape(rows, n_dp, n_mp, width_tile),...  29.1 us
    reshape x1, local copies, waits for them, and re-layouts, on_device(): gathered.reshape(rows, n_dp, n_mp, width_tile)  27.8 us
    psum x1, blocking collectives, on_device(): rank_output = lax.psum(partial_low, 'mp').astype(jnp.bfloat16)  16.2 us
    dot_general x1, matrix products, on_device(): jnp.dot(gathered, key_value_weight, preferred_element_type=jnp.float32)  15.6 us
  transfers between devices with their start and end apart: 3, of which 3 were waited for; matrix products, arithmetic and copies ran while one was open for 2% of the time, Pallas kernels for 0%

commit v1 on v0

--- a/solution.py
+++ b/solution.py
@@ -1,10 +1,18 @@
+import functools
+
 import jax
 import jax.numpy as jnp
+import numpy as np
 from jax import lax
+from jax.experimental import pallas as pl
+from jax.experimental.pallas import tpu as pltpu
 from jax.sharding import PartitionSpec as P
 
-
-def on_device(
+MESH = pl.DeviceIdType.MESH
+AHEAD = 6
+
+
+def plain(
     tokens,
     key_value_weight,
     adapter_down_weight,
@@ -50,6 +58,386 @@
     return (base + delta.reshape(rows, column_tile)).astype(jnp.bfloat16)
 
 
+def kernel(
+    n_dp,
+    sel,
+    target,
+    owner_adapter,
+    tok,
+    weight,
+    down,
+    up,
+    out,
+    t_all,
+    w_all,
+    d_all,
+    u_all,
+    acc,
+    part,
+    part_in,
+    swap_out,
+    swap_in,
+    low,
+    u_sel,
+    local_sem,
+    pair_send,
+    pair_recv,
+    y_send,
+    y_recv,
+    fwd_send,
+    fwd_recv,
+    d_send,
+    d_recv,
+    u_send,
+    u_recv,
+    hop_send,
+    hop_recv,
+):
+    group = lax.axis_index("dp")
+    me = lax.axis_index("mp")
+    y, core = me // 2, me % 2
+    other_y = 1 - y
+    sibling = y * 2 + (1 - core)
+    across = other_y * 2 + core
+    diagonal = other_y * 2 + (1 - core)
+
+    rows, depth = tok.shape
+    adapters, tile, double_rank = down.shape
+    rank = double_rank // 2
+    up_rows = up.shape[0]
+    pieces = 2 * n_dp
+    piece = 2 * tile
+    last = n_dp - 1
+    span = n_dp // 2
+    half_tile = tile // 2
+    half_adapters = adapters // 2
+
+    z, x = group // 2, group % 2
+    place = z + x * (n_dp - 1 - 2 * z)
+
+    def at_place(q):
+        q = (q + 2 * n_dp) % n_dp
+        side, step = q // span, q % span
+        return (step + side * (span - 1 - 2 * step)) * 2 + side
+
+    after, before = at_place(place + 1), at_place(place - 1)
+
+    barrier = pltpu.get_barrier_semaphore()
+    for partner in ((after, me), (before, me), (group, across), (group, sibling)):
+        pl.semaphore_signal(barrier, inc=1, device_id=partner, device_id_type=MESH)
+    pl.semaphore_wait(barrier, 4)
+
+    def remote(src, dst, send, recv, partner):
+        return pltpu.make_async_remote_copy(
+            src_ref=src, dst_ref=dst, send_sem=send, recv_sem=recv,
+            device_id=partner, device_id_type=MESH,
+        )
+
+    def d_part(ref, way, sub):
+        return ref.at[
+            pl.ds(sub * half_adapters, half_adapters), pl.ds(way * half_tile, half_tile)
+        ]
+
+    def sent_block(way, step):
+        return at_place(place - step) if way == 0 else at_place(place + step)
+
+    def d_copy(way, step, sub, block, src):
+        return remote(
+            d_part(src, way, sub), d_part(d_all.at[block], way, sub),
+            d_send.at[way, step, sub], d_recv.at[way, step, sub],
+            (after if way == 0 else before, me),
+        )
+
+    def u_copy(way, step, block, src, first):
+        half = up_rows // 2
+        there = pl.ds(pl.multiple_of(block * up_rows + way * half, half), half)
+        here = pl.ds(way * half, half) if first else there
+        return remote(
+            src.at[here], u_all.at[there],
+            u_send.at[way, step], u_recv.at[way, step],
+            (after if way == 0 else before, me),
+        )
+
+    def columns(i, side):
+        start = (i % n_dp) * (4 * tile) + ((side + i // n_dp) % 2) * piece
+        return pl.ds(pl.multiple_of(start, piece), piece)
+
+    def y_copy(i):
+        cols = columns(i, other_y)
+        return remote(
+            tok.at[:, cols], t_all.at[me, :, cols], y_send.at[i], y_recv.at[i], (group, across)
+        )
+
+    def y_arrival(i):
+        cols = columns(i, y)
+        return remote(
+            tok.at[:, cols], t_all.at[across, :, cols], y_send.at[i], y_recv.at[i],
+            (group, across),
+        )
+
+    def fwd_copy(i):
+        cols = columns(i, y)
+        return remote(
+            t_all.at[across, :, cols], t_all.at[across, :, cols],
+            fwd_send.at[i], fwd_recv.at[i], (group, sibling),
+        )
+
+    def fwd_arrival(i):
+        cols = columns(i, y)
+        return remote(
+            t_all.at[diagonal, :, cols], t_all.at[diagonal, :, cols],
+            fwd_send.at[i], fwd_recv.at[i], (group, sibling),
+        )
+
+    for sub in range(2):
+        for way in range(2):
+            d_copy(way, 0, sub, group, down).start()
+    for way in range(2):
+        u_copy(way, 0, group, up, True).start()
+    for i in range(AHEAD):
+        y_copy(i).start()
+    t_local = pltpu.make_async_copy(tok, t_all.at[me], local_sem.at[0])
+    w_local = pltpu.make_async_copy(weight, w_all, local_sem.at[1])
+    d_local = pltpu.make_async_copy(down, d_all.at[group], local_sem.at[2])
+    u_local = pltpu.make_async_copy(
+        up, u_all.at[pl.ds(pl.multiple_of(group * up_rows, up_rows), up_rows)], local_sem.at[3]
+    )
+    t_local.start()
+    w_local.start()
+    d_local.start()
+    u_local.start()
+    pair = remote(tok, t_all.at[me], pair_send, pair_recv, (group, sibling))
+    pair.start()
+
+    acc[...] = jnp.zeros_like(acc)
+
+    def add(block, cols):
+        acc[block] += jnp.dot(
+            t_all[block, :, cols], w_all[cols, :], preferred_element_type=jnp.float32
+        )
+
+    def add_whole(block):
+        @pl.loop(0, n_dp)
+        def _(k):
+            add(block, pl.ds(pl.multiple_of(k * 4 * tile, 4 * tile), 4 * tile))
+
+    t_local.wait()
+    w_local.wait()
+    add_whole(me)
+
+    def take_piece(i):
+        y_arrival(i).wait_recv()
+        fwd_copy(i).start()
+        y_copy(i).wait_send()
+
+        @pl.when(i + AHEAD < pieces)
+        def _():
+            y_copy(i + AHEAD).start()
+
+        add(across, columns(i, y))
+
+        @pl.when(i > 0)
+        def _():
+            fwd_arrival(i - 1).wait_recv()
+            add(diagonal, columns(i - 1, y))
+
+    @pl.loop(0, last)
+    def _(step):
+        for sub in range(2):
+            for way in range(2):
+                block = at_place(place - 1 - step) if way == 0 else at_place(place + 1 + step)
+                d_copy(way, step, sub, block, d_all.at[block]).wait_recv()
+
+                @pl.when(step + 1 < last)
+                def _():
+                    d_copy(way, step + 1, sub, block, d_all.at[block]).start()
+        for way in range(2):
+            block = at_place(place - 1 - step) if way == 0 else at_place(place + 1 + step)
+            u_copy(way, step, block, u_all, False).wait_recv()
+
+            @pl.when(step + 1 < last)
+            def _():
+                u_copy(way, step + 1, block, u_all, False).start()
+
+        @pl.when(step == 0)
+        def _():
+            remote(tok, t_all.at[sibling], pair_send, pair_recv, (group, sibling)).wait_recv()
+            add_whole(sibling)
+
+        @pl.when(step > 0)
+        def _():
+            @pl.loop(2 * step - 2, 2 * step)
+            def _(i):
+                take_piece(i)
+
+    d_local.wait()
+    u_local.wait()
+
+    segs = sel.shape[0]
+    seg_block = segs // 4
+    seg_len = rows // seg_block
+
+    def partial_low(c):
+        @pl.loop(0, 2 * seg_block)
+        def _(k):
+            yy, inner = k // seg_block, k % seg_block
+            block = yy * 2 + c
+            adapter = sel[block * seg_block + inner]
+            span_rows = pl.ds(pl.multiple_of(inner * seg_len, seg_len), seg_len)
+            total = jnp.zeros((seg_len, double_rank), jnp.float32)
+            for g in range(n_dp):
+                cols = pl.ds(pl.multiple_of(g * 4 * tile + me * tile, tile), tile)
+                total += jnp.dot(
+                    t_all[block, span_rows, cols], d_all[g, adapter],
+                    preferred_element_type=jnp.float32,
+                )
+            part[c, yy, span_rows, :] = total
+
+    partial_low(1 - core)
+    hop1 = remote(part.at[1 - core], part_in, hop_send.at[0], hop_recv.at[0], (group, sibling))
+    hop1.start()
+    partial_low(core)
+    hop1.wait_recv()
+    q0 = part[core, 0] + part_in[0]
+    q1 = part[core, 1] + part_in[1]
+    key_part = jnp.concatenate([q0[:, :rank], q1[:, :rank]], axis=1)
+    value_part = jnp.concatenate([q0[:, rank:], q1[:, rank:]], axis=1)
+    swap_out[0] = jnp.where(y == 0, value_part, key_part)
+    swap_out[1] = jnp.where(y == 0, key_part, value_part)
+    hop2 = remote(swap_out.at[0], swap_in, hop_send.at[1], hop_recv.at[1], (group, across))
+    hop2.start()
+
+    @pl.loop(0, segs)
+    def _(s):
+        yy = s // (2 * seg_block)
+        line = lax.broadcasted_iota(jnp.int32, (double_rank, u_all.shape[0]), 0)
+        hit = (line == target[...] + yy * rank) & (owner_adapter[...] == sel[s])
+        pick = jnp.where(hit, 1.0, 0.0).astype(jnp.bfloat16)
+        u_sel[s] = jnp.dot(pick, u_all[...], preferred_element_type=jnp.float32).astype(
+            jnp.bfloat16
+        )
+
+    @pl.loop(2 * (last - 1), pieces)
+    def _(i):
+        take_piece(i)
+
+    hop2.wait_recv()
+    low[core] = (swap_out[1] + swap_in[...]).astype(jnp.bfloat16)
+    hop3 = remote(low.at[core], low.at[core], hop_send.at[2], hop_recv.at[2], (group, sibling))
+    hop3.start()
+    fwd_arrival(pieces - 1).wait_recv()
+    add(diagonal, columns(pieces - 1, y))
+
+    def finish(c):
+        @pl.loop(0, 2 * seg_block)
+        def _(k):
+            yy, inner = k // seg_block, k % seg_block
+            block = yy * 2 + c
+            span_rows = pl.ds(pl.multiple_of(inner * seg_len, seg_len), seg_len)
+            delta = jnp.dot(
+                low[c, span_rows, :], u_sel[block * seg_block + inner],
+                preferred_element_type=jnp.float32,
+            )
+            out[block, span_rows, :] = (acc[block, span_rows, :] + delta).astype(jnp.bfloat16)
+
+    finish(core)
+    remote(
+        low.at[1 - core], low.at[1 - core], hop_send.at[2], hop_recv.at[2], (group, sibling)
+    ).wait_recv()
+    finish(1 - core)
+
+    pair.wait_send()
+    hop1.wait_send()
+    hop2.wait_send()
+    hop3.wait_send()
+
+    @pl.loop(0, pieces)
+    def _(i):
+        fwd_copy(i).wait_send()
+
+    @pl.loop(0, last)
+    def _(step):
+        for way in range(2):
+            block = sent_block(way, step)
+            for sub in range(2):
+                d_copy(way, step, sub, block, d_all.at[block]).wait_send()
+            u_copy(way, step, block, u_all, False).wait_send()
+
+
+def on_device(
+    tokens,
+    key_value_weight,
+    adapter_down_weight,
+    adapter_up_weight,
+    adapter_per_request,
+    request_per_segment,
+):
+    n_dp = lax.axis_size("dp")
+    n_mp = lax.axis_size("mp")
+    rows, depth = tokens.shape
+    width = key_value_weight.shape[1]
+    adapters, tile, double_rank = adapter_down_weight.shape
+    up_rank = adapter_up_weight.shape[1]
+    if n_mp != 4 or tile % 256 or (adapters * up_rank) % 32 or n_dp % 2:
+        return plain(
+            tokens, key_value_weight, adapter_down_weight, adapter_up_weight,
+            adapter_per_request, request_per_segment,
+        )
+    seg_group = request_per_segment.shape[0] // n_dp
+    mine = lax.dynamic_slice_in_dim(
+        request_per_segment, lax.axis_index("dp") * seg_group, seg_group
+    )
+    sel = jnp.take(adapter_per_request, mine, axis=0)
+    up_rows = adapters * up_rank
+    index = np.arange(n_dp * up_rows)
+    target = jnp.asarray((index // up_rows * up_rank + index % up_rank)[None], jnp.int32)
+    owner_adapter = jnp.asarray((index // up_rank % adapters)[None], jnp.int32)
+    last = n_dp - 1
+    bf16, f32 = jnp.bfloat16, jnp.float32
+    dma = pltpu.SemaphoreType.DMA
+    vmem = pl.BlockSpec(memory_space=pltpu.VMEM)
+    result = pl.pallas_call(
+        functools.partial(kernel, n_dp),
+        out_shape=jax.ShapeDtypeStruct((n_mp, rows, width), bf16),
+        in_specs=[pl.BlockSpec(memory_space=pltpu.SMEM), vmem, vmem]
+        + [pl.BlockSpec(memory_space=pl.ANY)] * 4,
+        out_specs=vmem,
+        scratch_shapes=[
+            pltpu.VMEM((n_mp, rows, depth), bf16),
+            pltpu.VMEM((depth, width), bf16),
+            pltpu.VMEM((n_dp, adapters, tile, double_rank), bf16),
+            pltpu.VMEM((n_dp * up_rows, width), bf16),
+            pltpu.VMEM((n_mp, rows, width), f32),
+            pltpu.VMEM((2, 2, rows, double_rank), f32),
+            pltpu.VMEM((2, rows, double_rank), f32),
+            pltpu.VMEM((2, rows, double_rank), f32),
+            pltpu.VMEM((rows, double_rank), f32),
+            pltpu.VMEM((2, rows, double_rank), bf16),
+            pltpu.VMEM((seg_group, double_rank, width), bf16),
+            dma((4,)),
+            dma,
+            dma,
+            dma((2 * n_dp,)),
+            dma((2 * n_dp,)),
+            dma((2 * n_dp,)),
+            dma((2 * n_dp,)),
+            dma((2, last, 2)),
+            dma((2, last, 2)),
+            dma((2, last)),
+            dma((2, last)),
+            dma((3,)),
+            dma((3,)),
+        ],
+        compiler_params=pltpu.CompilerParams(
+            collective_id=0, has_side_effects=True, vmem_limit_bytes=52 * 2**20
+        ),
+    )(
+        sel, target, owner_adapter, tokens, key_value_weight, adapter_down_weight,
+        adapter_up_weight.reshape(up_rows, width),
+    )
+    return result.reshape(n_mp * rows, width)
+
+
 def solution(mesh):
     placed = (
         P(("dp", "mp"), None),

time: 393 us -> 114 us (0.29)
  waiting for transfers between devices: 267 us -> 0 us
  Pallas kernels: 0 us -> 108 us
  local copies, waits for them, and re-layouts: 73.4 us -> 3.9 us
  matrix products: 21.1 us -> 0 us
  blocking collectives: 16.2 us -> 0 us
  between operations: 13.2 us -> 0.02 us
    all_gather x3 -> x0, waiting for transfers between devices: 265 us -> none  [the longest x1 124 us: on_device(): lax.all_gather(adapter_down_weight, 'dp', axis=1, tiled=True)]
    pallas_call x0 -> x1, Pallas kernels: none -> 108 us  [on_device(): pl.pallas_call(functools.partial(kernel, n_dp), out_shape=jax.ShapeDtypeS...]
    reshape x2 -> x0, local copies, waits for them, and re-layouts: 35.2 us -> none  [the longest x1 27.8 us: on_device(): gathered.reshape(rows, n_dp, n_mp, width_tile)]
    dynamic_slice x1 -> x0, local copies, waits for them, and re-layouts: 29.1 us -> none  [on_device(): lax.dynamic_index_in_dim(gathered.reshape(rows, n_dp, n_mp, width_tile),...]
    dot_general x3 -> x0, matrix products: 21.1 us -> none  [the longest x1 15.6 us: on_device(): jnp.dot(gathered, key_value_weight, preferred_element_type=jnp.float32)]
    psum x1 -> x0, blocking collectives: 16.2 us -> none  [on_device(): rank_output = lax.psum(partial_low, 'mp').astype(jnp.bfloat16)]
    gather x3 -> x1, local copies, waits for them, and re-layouts: 9.12 us -> 0.64 us  [on_device(): sel = jnp.take(adapter_per_request, mine, axis=0)]
  transfers between devices with their start and end apart: 3 -> 0, of which waited for: 3 -> 0; matrix products, arithmetic and copies ran while one was open for 2% -> 0% of each run, Pallas kernels for 0% -> 0%
where the time goes in v1:
time: 114 us; the launch traced here: 113 us
  Pallas kernels  108 us (95%)
  local copies, waits for them, and re-layouts  3.9 us (3%)
  other arithmetic  1.49 us (1%)
    pallas_call x1, Pallas kernels, on_device(): pl.pallas_call(functools.partial(kernel, n_dp), out_shape=jax.ShapeDtypeS...  108 us
    unnamed x9, local copies, waits for them, and re-layouts  3.25 us

profile of v1, /device:TPU:0, one launch (start us, length us, event | category | flops | bytes accessed | tf_op | source)
XLA Modules:
  0.0 113.3 jit_solution(8513544608048092157)
XLA Ops:
  0.0 0.0 copy-start
  0.0 0.7 compare_select_fusion
  0.8 0.0 copy-done
  0.8 0.6 gather_fusion
  1.4 0.7 and_select_fusion.sel
  2.1 0.0 copy-start.1
  2.1 0.9 copy-done.1
  3.0 0.0 copy-start.2
  3.0 0.7 copy-done.2
  3.7 0.0 copy-start.3
  3.7 0.7 copy-done.3
  4.4 107.9 %shard_map.82 = bf16[4,256,512]{2,1,0:T(8,128)(2,1)S(1)} custom-call(s32[8]{0:T(128)S(1)} %and_select_fusion.sel, s32[1,1024]{1,0:T(1,128)S(1)} %copy-done.3, s32[1,1024]{1,0:T(1,128)S(1)} %copy-done.2, bf16[256,8192]{1,0:T(8,128)(2,1)} %tok.1, bf16[8192,512]{1,0:T(8,128)(2,1)} %weight.1, bf16[16,256,128]{2,1,0:T(8,128)(2,1)} %down.1, ...), custom_call_target="tpu_custom_call" | custom-call | tf_op jit(solution)/shard_map/pallas_call | solution.py:399
  112.4 1.0 copy.10
  (1 shorter events, 0.0 us)
Async XLA Ops:
  0.0 0.8 copy-start
  2.1 0.9 copy-start.1
  3.0 0.7 copy-start.2
  3.7 0.7 copy-start.3

commit v2 on v1

v2 whole, which is shorter than its diff:
```python
import functools

import jax
import jax.numpy as jnp
from jax import lax
from jax.experimental import pallas as pl
from jax.experimental.pallas import tpu as pltpu
from jax.sharding import PartitionSpec as P

MESH = pl.DeviceIdType.MESH
AHEAD = 4


def plain(
    tokens,
    key_value_weight,
    adapter_down_weight,
    adapter_up_weight,
    adapter_per_request,
    request_per_segment,
):
    n_dp = lax.axis_size("dp")
    n_mp = lax.axis_size("mp")
    group = lax.axis_index("dp")
    column = lax.axis_index("mp")
    seg_total = request_per_segment.shape[0]
    seg_group = seg_total // n_dp
    seg_adapter = jnp.take(adapter_per_request, request_per_segment, axis=0)
    local_portion = lax.dynamic_slice_in_dim(seg_adapter, group * seg_group, seg_group)
    gathered = lax.all_gather(tokens, "mp", axis=0, tiled=True)
    rows = gathered.shape[0]
    seg_len = rows // seg_group
    width_tile = adapter_down_weight.shape[1]
    double_rank = adapter_down_weight.shape[2]
    rank = double_rank // 2
    column_tile = adapter_up_weight.shape[2]
    base = jnp.dot(gathered, key_value_weight, preferred_element_type=jnp.float32)
    strided = lax.dynamic_index_in_dim(
        gathered.reshape(rows, n_dp, n_mp, width_tile), column, 2, keepdims=False
    ).reshape(seg_group, seg_len, n_dp * width_tile)
    selected_factor = jnp.take(
        lax.all_gather(adapter_down_weight, "dp", axis=1, tiled=True), local_portion, axis=0
    )
    partial_low = jnp.einsum(
        "sti,sir->str", strided, selected_factor, preferred_element_type=jnp.float32
    )
    selected_factor = jnp.take(
        lax.all_gather(adapter_up_weight, "dp", axis=1, tiled=True), local_portion, axis=0
    )
    rank_output = lax.psum(partial_low, "mp").astype(jnp.bfloat16)
    key_width = n_mp * column_tile // 2
    half = column * column_tile // key_width
    low_half = lax.dynamic_slice_in_dim(rank_output, half * rank, rank, 2)
    delta = jnp.einsum(
        "str,src->stc", low_half, selected_factor, preferred_element_type=jnp.float32
    )
    return (base + delta.reshape(rows, column_tile)).astype(jnp.bfloat16)


def kernel(
    n_dp,
    up_rank,
    requests,
    segments,
    tok,
    weight,
    down,
    up,
    out,
    t_all,
    w_all,
    d_own,
    d_one,
    d_two,
    d_three,
    d_three_picked,
    d_four_picked,
    stage_three,
    stage_four,
    u_all,
    acc,
    part,
    part_in,
    swap_out,
    swap_in,
    low,
    u_sel,
    local_sem,
    pair_send,
    pair_recv,
    y_send,
    y_recv,
    fwd_send,
    fwd_recv,
    d_send,
    d_recv,
    u_send,
    u_recv,
    hop_send,
    hop_recv,
):
    group = lax.axis_index("dp")
    me = lax.axis_index("mp")
    y, core = me // 2, me % 2
    other_y = 1 - y
    sibling = y * 2 + (1 - core)
    across = other_y * 2 + core
    diagonal = other_y * 2 + (1 - core)

    rows, depth = tok.shape
    adapters, tile, double_rank = down.shape
    rank = double_rank // 2
    up_rows = up.shape[0]
    pieces = 2 * n_dp
    piece = 2 * tile
    span = n_dp // 2
    half_tile = tile // 2
    quarter = adapters // 4
    segs = segments.shape[0] // n_dp
    seg_block = segs // 4
    seg_len = rows // seg_block

    z, x = group // 2, group % 2
    place = z + x * (n_dp - 1 - 2 * z)

    def at_place(q):
        q = (q + 2 * n_dp) % n_dp
        side, step = q // span, q % span
        return (step + side * (span - 1 - 2 * step)) * 2 + side

    after, before = at_place(place + 1), at_place(place - 1)
    onward = (after, before)

    def adapter_of(g, seg):
        return requests[segments[g * segs + seg]]

    barrier = pltpu.get_barrier_semaphore()
    for partner in ((after, me), (before, me), (group, across), (group, sibling)):
        pl.semaphore_signal(barrier, inc=1, device_id=partner, device_id_type=MESH)
    pl.semaphore_wait(barrier, 4)

    def remote(src, dst, send, recv, partner):
        return pltpu.make_async_remote_copy(
            src_ref=src, dst_ref=dst, send_sem=send, recv_sem=recv,
            device_id=partner, device_id_type=MESH,
        )

    def quarter_of(k):
        return pl.ds(k * quarter, quarter)

    def one(way, k):
        return remote(
            down.at[quarter_of(k)], d_one.at[way, quarter_of(k)],
            d_send.at[way, k], d_recv.at[way, k], (onward[way], me),
        )

    def two(way, k):
        return remote(
            d_one.at[way, quarter_of(k)], d_two.at[way, quarter_of(k)],
            d_send.at[way, 4 + k], d_recv.at[way, 4 + k], (onward[way], me),
        )

    def three(way, k):
        return remote(
            d_two.at[way, quarter_of(k), pl.ds(way * half_tile, half_tile)],
            d_three.at[way, quarter_of(k)],
            d_send.at[way, 8 + k], d_recv.at[way, 8 + k], (onward[way], me),
        )

    def three_picked(way):
        return remote(
            stage_three.at[way], d_three_picked.at[way],
            d_send.at[way, 12], d_recv.at[way, 12], (onward[way], me),
        )

    def four_picked(way):
        return remote(
            stage_four.at[way], d_four_picked.at[way],
            d_send.at[way, 13], d_recv.at[way, 13], (onward[way], me),
        )

    def u_rows(way, step, block):
        if step < span - 1:
            return pl.ds(pl.multiple_of(block * up_rows, up_rows), up_rows)
        half = up_rows // 2
        return pl.ds(pl.multiple_of(block * up_rows + way * half, half), half)

    def u_copy(way, step):
        block = at_place(place - step) if way == 0 else at_place(place + step)
        there = u_rows(way, step, block)
        return remote(
            up if step == 0 else u_all.at[there], u_all.at[there],
            u_send.at[way, step], u_recv.at[way, step], (onward[way], me),
        )

    def u_arrival(way, step):
        block = at_place(place - 1 - step) if way == 0 else at_place(place + 1 + step)
        there = u_rows(way, step, block)
        return remote(
            u_all.at[there], u_all.at[there],
            u_send.at[way, step], u_recv.at[way, step], (onward[way], me),
        )

    def near(k):
        return at_place(place + (k + 1) // 2 * (1 - 2 * (k % 2)))

    def columns(i, side):
        start = near(i % n_dp) * (4 * tile) + ((side + i // n_dp) % 2) * piece
        return pl.ds(pl.multiple_of(start, piece), piece)

    def y_copy(i):
        cols = columns(i, other_y)
        return remote(
            tok.at[:, cols], t_all.at[me, :, cols], y_send.at[i], y_recv.at[i], (group, across)
        )

    def y_arrival(i):
        cols = columns(i, y)
        return remote(
            tok.at[:, cols], t_all.at[across, :, cols], y_send.at[i], y_recv.at[i],
            (group, across),
        )

    def fwd_copy(i):
        cols = columns(i, y)
        return remote(
            t_all.at[across, :, cols], t_all.at[across, :, cols],
            fwd_send.at[i], fwd_recv.at[i], (group, sibling),
        )

    def fwd_arrival(i):
        cols = columns(i, y)
        return remote(
            t_all.at[diagonal, :, cols], t_all.at[diagonal, :, cols],
            fwd_send.at[i], fwd_recv.at[i], (group, sibling),
        )

    for i in range(AHEAD):
        y_copy(i).start()
    for k in range(4):
        for way in range(2):
            one(way, k).start()
    for way in range(2):
        u_copy(way, 0).start()
    t_local = pltpu.make_async_copy(tok, t_all.at[me], local_sem.at[0])
    w_local = pltpu.make_async_copy(weight, w_all, local_sem.at[1])
    d_local = pltpu.make_async_copy(down, d_own, local_sem.at[2])
    u_local = pltpu.make_async_copy(
        up, u_all.at[pl.ds(pl.multiple_of(group * up_rows, up_rows), up_rows)], local_sem.at[3]
    )
    t_local.start()
    w_local.start()
    d_local.start()
    u_local.start()
    pair = remote(tok, t_all.at[me], pair_send, pair_recv, (group, sibling))
    pair.start()

    acc[...] = jnp.zeros_like(acc)
    part[...] = jnp.zeros_like(part)

    def add(block, cols):
        acc[block] += jnp.dot(
            t_all[block, :, cols], w_all[cols, :], preferred_element_type=jnp.float32
        )

    def add_whole(block):
        @pl.loop(0, n_dp)
        def _(k):
            add(block, pl.ds(pl.multiple_of(k * 4 * tile, 4 * tile), 4 * tile))

    def take_piece(i):
        y_arrival(i).wait_recv()
        fwd_copy(i).start()
        y_copy(i).wait_send()

        @pl.when(i + AHEAD < pieces)
        def _():
            y_copy(i + AHEAD).start()

        add(across, columns(i, y))

        @pl.when(i > 0)
        def _():
            fwd_arrival(i - 1).wait_recv()
            add(diagonal, columns(i - 1, y))

    def add_low(blocks, factors):
        @pl.loop(0, segs)
        def _(s):
            block, inner = s // seg_block, s % seg_block
            span_rows = pl.ds(pl.multiple_of(inner * seg_len, seg_len), seg_len)
            adapter = adapter_of(group, s)
            total = part[block % 2, block // 2, span_rows, :]
            for g, factor in zip(blocks, factors):
                cols = pl.ds(pl.multiple_of(g * 4 * tile + me * tile, tile), tile)
                total += jnp.dot(
                    t_all[block, span_rows, cols], factor(adapter, s),
                    preferred_element_type=jnp.float32,
                )
            part[block % 2, block // 2, span_rows, :] = total

    t_local.wait()
    w_local.wait()
    add_whole(me)

    @pl.loop(0, 4)
    def _(k):
        for way in range(2):
            one(way, k).wait_recv()
            two(way, k).start()

        @pl.when(k == 1)
        def _():
            remote(tok, t_all.at[sibling], pair_send, pair_recv, (group, sibling)).wait_recv()
            add_whole(sibling)

        @pl.when(k > 0)
        def _():
            take_piece(k - 1)

    for way in range(2):
        u_arrival(way, 0).wait_recv()
        u_copy(way, 1).start()
    d_local.wait()
    u_local.wait()

    @pl.loop(0, 4)
    def _(k):
        for way in range(2):
            two(way, k).wait_recv()
            three(way, k).start()
        take_piece(k + 3)

        @pl.when(k == 1)
        def _():
            add_low(
                [group, before, after],
                [lambda a, s: d_own[a], lambda a, s: d_one[0, a], lambda a, s: d_one[1, a]],
            )

    @pl.loop(0, segs)
    def _(s):
        for way in range(2):
            stage_three[way, s] = d_two[
                way, adapter_of(onward[way], s), pl.ds((1 - way) * half_tile, half_tile), :
            ]

    for way in range(2):
        three_picked(way).start()
    for way in range(2):
        u_arrival(way, 1).wait_recv()
        u_copy(way, 2).start()
    add_low(
        [at_place(place - 2), at_place(place + 2)],
        [lambda a, s: d_two[0, a], lambda a, s: d_two[1, a]],
    )

    @pl.loop(0, 2)
    def _(h):
        take_piece(h + 7)
        for j in range(2):
            for way in range(2):
                three(way, 2 * h + j).wait_recv()

    @pl.loop(0, segs)
    def _(s):
        for way in range(2):
            stage_four[way, s] = d_three[way, adapter_of(onward[way], s)]

    for way in range(2):
        four_picked(way).start()
    for way in range(2):
        u_arrival(way, 2).wait_recv()
        u_copy(way, 3).start()
    take_piece(9)
    for way in range(2):
        three_picked(way).wait_recv()
    add_low(
        [at_place(place - 3), at_place(place + 3)],
        [
            lambda a, s: jnp.concatenate([d_three[0, a], d_three_picked[0, s]], axis=0),
            lambda a, s: jnp.concatenate([d_three_picked[1, s], d_three[1, a]], axis=0),
        ],
    )
    take_piece(10)
    for way in range(2):
        four_picked(way).wait_recv()
    add_low(
        [at_place(place + 4)],
        [lambda a, s: jnp.concatenate([d_four_picked[0, s], d_four_picked[1, s]], axis=0)],
    )

    hop1 = remote(part.at[1 - core], part_in, hop_send.at[0], hop_recv.at[0], (group, sibling))
    hop1.start()
    hop1.wait_recv()
    q0 = part[core, 0] + part_in[0]
    q1 = part[core, 1] + part_in[1]
    key_part = jnp.concatenate([q0[:, :rank], q1[:, :rank]], axis=1)
    value_part = jnp.concatenate([q0[:, rank:], q1[:, rank:]], axis=1)
    swap_out[0] = jnp.where(y == 0, value_part, key_part)
    swap_out[1] = jnp.where(y == 0, key_part, value_part)
    hop2 = remote(swap_out.at[0], swap_in, hop_send.at[1], hop_recv.at[1], (group, across))
    hop2.start()

    for way in range(2):
        u_arrival(way, 3).wait_recv()

    total_rows = u_all.shape[0]
    index = lax.broadcasted_iota(jnp.int32, (1, total_rows), 1)
    by_group, by_adapter = up_rows.bit_length() - 1, up_rank.bit_length() - 1
    target = lax.shift_right_logical(index, by_group) * up_rank + (index & (up_rank - 1))
    holder = lax.shift_right_logical(index, by_adapter) & (adapters - 1)

    @pl.loop(0, segs)
    def _(s):
        yy = s // (2 * seg_block)
        line = lax.broadcasted_iota(jnp.int32, (double_rank, total_rows), 0)
        hit = (line == target + yy * rank) & (holder == adapter_of(group, s))
        pick = jnp.where(hit, 1.0, 0.0).astype(jnp.bfloat16)
        u_sel[s] = jnp.dot(pick, u_all[...], preferred_element_type=jnp.float32).astype(
            jnp.bfloat16
        )

    @pl.loop(11, pieces - 2)
    def _(i):
        take_piece(i)

    hop2.wait_recv()
    low[core] = (swap_out[1] + swap_in[...]).astype(jnp.bfloat16)
    hop3 = remote(low.at[core], low.at[core], hop_send.at[2], hop_recv.at[2], (group, sibling))
    hop3.start()
    take_piece(pieces - 2)
    remote(
        low.at[1 - core], low.at[1 - core], hop_send.at[2], hop_recv.at[2], (group, sibling)
    ).wait_recv()

    @pl.loop(0, segs)
    def _(s):
        block, inner = s // seg_block, s % seg_block
        span_rows = pl.ds(pl.multiple_of(inner * seg_len, seg_len), seg_len)
        acc[block, span_rows, :] += jnp.dot(
            low[block % 2, span_rows, :], u_sel[s], preferred_element_type=jnp.float32
        )

    out[me] = acc[me].astype(jnp.bfloat16)
    out[sibling] = acc[sibling].astype(jnp.bfloat16)
    take_piece(pieces - 1)
    out[across] = acc[across].astype(jnp.bfloat16)
    fwd_arrival(pieces - 1).wait_recv()
    add(diagonal, columns(pieces - 1, y))
    out[diagonal] = acc[diagonal].astype(jnp.bfloat16)

    pair.wait_send()
    hop1.wait_send()
    hop2.wait_send()
    hop3.wait_send()

    @pl.loop(0, pieces)
    def _(i):
        fwd_copy(i).wait_send()

    for way in range(2):
        for k in range(4):
            one(way, k).wait_send()
            two(way, k).wait_send()
            three(way, k).wait_send()
        three_picked(way).wait_send()
        four_picked(way).wait_send()
        for step in range(4):
            u_copy(way, step).wait_send()


def on_device(
    tokens,
    key_value_weight,
    adapter_down_weight,
    adapter_up_weight,
    adapter_per_request,
    request_per_segment,
):
    n_dp = lax.axis_size("dp")
    n_mp = lax.axis_size("mp")
    rows, depth = tokens.shape
    width = key_value_weight.shape[1]
    adapters, tile, double_rank = adapter_down_weight.shape
    up_rank = adapter_up_weight.shape[1]
    whole_tiles = tile % 256 == 0 and adapters % 4 == 0 and (adapters * up_rank) % 32 == 0
    powers = adapters & (adapters - 1) == 0 and up_rank & (up_rank - 1) == 0
    if n_mp != 4 or n_dp != 8 or not whole_tiles or not powers:
        return plain(
            tokens, key_value_weight, adapter_down_weight, adapter_up_weight,
            adapter_per_request, request_per_segment,
        )
    seg_group = request_per_segment.shape[0] // n_dp
    up_rows = adapters * up_rank
    bf16, f32 = jnp.bfloat16, jnp.float32
    dma = pltpu.SemaphoreType.DMA
    vmem = pl.BlockSpec(memory_space=pltpu.VMEM)
    result = pl.pallas_call(
        functools.partial(kernel, n_dp, up_rank),
        out_shape=jax.ShapeDtypeStruct((n_mp, rows, width), bf16),
        in_specs=[pl.BlockSpec(memory_space=pltpu.SMEM)] * 2
        + [pl.BlockSpec(memory_space=pl.ANY)] * 4,
        out_specs=vmem,
        scratch_shapes=[
            pltpu.VMEM((n_mp, rows, depth), bf16),
            pltpu.VMEM((depth, width), bf16),
            pltpu.VMEM((adapters, tile, double_rank), bf16),
            pltpu.VMEM((2, adapters, tile, double_rank), bf16),
            pltpu.VMEM((2, adapters, tile, double_rank), bf16),
            pltpu.VMEM((2, adapters, tile // 2, double_rank), bf16),
            pltpu.VMEM((2, seg_group, tile // 2, double_rank), bf16),
            pltpu.VMEM((2, seg_group, tile // 2, double_rank), bf16),
            pltpu.VMEM((2, seg_group, tile // 2, double_rank), bf16),
            pltpu.VMEM((2, seg_group, tile // 2, double_rank), bf16),
            pltpu.VMEM((n_dp * up_rows, width), bf16),
            pltpu.VMEM((n_mp, rows, width), f32),
            pltpu.VMEM((2, 2, rows, double_rank), f32),
            pltpu.VMEM((2, rows, double_rank), f32),
            pltpu.VMEM((2, rows, double_rank), f32),
            pltpu.VMEM((rows, double_rank), f32),
            pltpu.VMEM((2, rows, double_rank), bf16),
            pltpu.VMEM((seg_group, double_rank, width), bf16),
            dma((4,)),
            dma,
            dma,
            dma((2 * n_dp,)),
            dma((2 * n_dp,)),
            dma((2 * n_dp,)),
            dma((2 * n_dp,)),
            dma((2, 14)),
            dma((2, 14)),
            dma((2, 4)),
            dma((2, 4)),
            dma((3,)),
            dma((3,)),
        ],
        compiler_params=pltpu.CompilerParams(
            collective_id=0, has_side_effects=True, vmem_limit_bytes=52 * 2**20
        ),
    )(
        adapter_per_request, request_per_segment, tokens, key_value_weight, adapter_down_weight,
        adapter_up_weight.reshape(up_rows, width),
    )
    return result.reshape(n_mp * rows, width)


def solution(mesh):
    placed = (
        P(("dp", "mp"), None),
        P(None, "mp"),
        P(None, ("dp", "mp"), None),
        P(None, "dp", "mp"),
        P(),
        P(),
    )
    return jax.shard_map(
        on_device, mesh=mesh, in_specs=placed, out_specs=P("dp", "mp"), check_vma=False
    )
```

time: 114 us -> 105 us (0.921)
  Pallas kernels: 108 us -> 101 us
  other arithmetic: 1.49 us -> 0 us
    pallas_call x1, Pallas kernels: 108 us -> 101 us  [on_device(): pl.pallas_call(functools.partial(kernel, n_dp, up_rank), out_shape=jax.Sh...]
    select_n x2 -> x0, other arithmetic: 1.48 us -> none  [on_device(): sel = jnp.take(adapter_per_request, mine, axis=0)]
    unnamed x9 -> x7, local copies, waits for them, and re-layouts: 3.25 us -> 3.19 us
where the time goes in v2:
time: 105 us; the launch traced here: 104 us
  Pallas kernels  101 us (96%)
  local copies, waits for them, and re-layouts  3.19 us (3%)
    pallas_call x1, Pallas kernels, on_device(): pl.pallas_call(functools.partial(kernel, n_dp, up_rank), out_shape=jax.Sh...  101 us
    unnamed x7, local copies, waits for them, and re-layouts  3.19 us

profile of v2, /device:TPU:0, one launch (start us, length us, event | category | flops | bytes accessed | tf_op | source)
XLA Modules:
  0.0 104.2 jit_solution(6233381241780833315)
XLA Ops:
  0.0 0.0 copy-start
  0.0 0.9 copy-done
  0.9 0.0 copy-start.1
  0.9 0.7 copy-done.1
  1.6 0.0 copy-start.2
  1.6 0.7 copy-done.2
  2.2 101.0 %shard_map.64 = bf16[4,256,512]{2,1,0:T(8,128)(2,1)S(1)} custom-call(s32[32]{0:T(128)S(1)} %copy-done.1, s32[64]{0:T(128)S(1)} %copy-done.2, bf16[256,8192]{1,0:T(8,128)(2,1)} %tok.1, bf16[8192,512]{1,0:T(8,128)(2,1)} %weight.1, bf16[16,256,128]{2,1,0:T(8,128)(2,1)} %down.1, bf16[128,512]{1,0:T(8,128)(2,1)S(1)} %bitcast.3), custom_call_target="tpu_custom_call" | custom-call | tf_op jit(solution)/shard_map/pallas_call | solution.py:499
  103.2 1.0 copy.8
Async XLA Ops:
  0.0 0.9 copy-start
  0.9 0.7 copy-start.1
  1.6 0.7 copy-start.2

commit v3 on v2

--- a/solution.py
+++ b/solution.py
@@ -8,7 +8,7 @@
 from jax.sharding import PartitionSpec as P
 
 MESH = pl.DeviceIdType.MESH
-AHEAD = 4
+AHEAD = 6
 
 
 def plain(
@@ -240,8 +240,6 @@
     for k in range(4):
         for way in range(2):
             one(way, k).start()
-    for way in range(2):
-        u_copy(way, 0).start()
     t_local = pltpu.make_async_copy(tok, t_all.at[me], local_sem.at[0])
     w_local = pltpu.make_async_copy(weight, w_all, local_sem.at[1])
     d_local = pltpu.make_async_copy(down, d_own, local_sem.at[2])
@@ -273,7 +271,7 @@
         fwd_copy(i).start()
         y_copy(i).wait_send()
 
-        @pl.when(i + AHEAD < pieces)
+        @pl.when(i + AHEAD < pieces - 1)
         def _():
             y_copy(i + AHEAD).start()
 
@@ -318,9 +316,6 @@
         def _():
             take_piece(k - 1)
 
-    for way in range(2):
-        u_arrival(way, 0).wait_recv()
-        u_copy(way, 1).start()
     d_local.wait()
     u_local.wait()
 
@@ -347,9 +342,6 @@
 
     for way in range(2):
         three_picked(way).start()
-    for way in range(2):
-        u_arrival(way, 1).wait_recv()
-        u_copy(way, 2).start()
     add_low(
         [at_place(place - 2), at_place(place + 2)],
         [lambda a, s: d_two[0, a], lambda a, s: d_two[1, a]],
@@ -370,8 +362,7 @@
     for way in range(2):
         four_picked(way).start()
     for way in range(2):
-        u_arrival(way, 2).wait_recv()
-        u_copy(way, 3).start()
+        u_copy(way, 0).start()
     take_piece(9)
     for way in range(2):
         three_picked(way).wait_recv()
@@ -392,6 +383,9 @@
 
     hop1 = remote(part.at[1 - core], part_in, hop_send.at[0], hop_recv.at[0], (group, sibling))
     hop1.start()
+    for way in range(2):
+        u_arrival(way, 0).wait_recv()
+        u_copy(way, 1).start()
     hop1.wait_recv()
     q0 = part[core, 0] + part_in[0]
     q1 = part[core, 1] + part_in[1]
@@ -401,7 +395,17 @@
     swap_out[1] = jnp.where(y == 0, key_part, value_part)
     hop2 = remote(swap_out.at[0], swap_in, hop_send.at[1], hop_recv.at[1], (group, across))
     hop2.start()
-
+    y_copy(pieces - 1).start()
+
+    take_piece(11)
+    for way in range(2):
+        u_arrival(way, 1).wait_recv()
+        u_copy(way, 2).start()
+    take_piece(12)
+    for way in range(2):
+        u_arrival(way, 2).wait_recv()
+        u_copy(way, 3).start()
+    take_piece(13)
     for way in range(2):
         u_arrival(way, 3).wait_recv()
 
@@ -420,10 +424,6 @@
         u_sel[s] = jnp.dot(pick, u_all[...], preferred_element_type=jnp.float32).astype(
             jnp.bfloat16
         )
-
-    @pl.loop(11, pieces - 2)
-    def _(i):
-        take_piece(i)
 
     hop2.wait_recv()
     low[core] = (swap_out[1] + swap_in[...]).astype(jnp.bfloat16)
@@ -536,7 +536,7 @@
             dma((3,)),
         ],
         compiler_params=pltpu.CompilerParams(
-            collective_id=0, has_side_effects=True, vmem_limit_bytes=52 * 2**20
+            collective_id=0, has_side_effects=True, vmem_limit_bytes=63 * 2**20
         ),
     )(
         adapter_per_request, request_per_segment, tokens, key_value_weight, adapter_down_weight,

time: 105 us -> 105 us (level)
    pallas_call x1, Pallas kernels: 101 us -> 102 us  [on_device(): pl.pallas_call(functools.partial(kernel, n_dp, up_rank), out_shape=jax.Sh...]
    unnamed x7 -> x1, local copies, waits for them, and re-layouts: 3.19 us -> 2.26 us
where the time goes in v3:
time: 105 us; the launch traced here: 104 us
  Pallas kernels  102 us (97%)
  local copies, waits for them, and re-layouts  2.26 us (2%)
    pallas_call x1, Pallas kernels, on_device(): pl.pallas_call(functools.partial(kernel, n_dp, up_rank), out_shape=jax.Sh...  102 us
    unnamed x1, local copies, waits for them, and re-layouts  2.26 us

profile of v3, /device:TPU:0, one launch (start us, length us, event | category | flops | bytes accessed | tf_op | source)
XLA Modules:
  0.0 104.4 jit_solution(8077080954023144845)
XLA Ops:
  0.0 102.1 %shard_map.64 = bf16[4,256,512]{2,1,0:T(8,128)(2,1)} custom-call(s32[32]{0:T(128)} %requests.1, s32[64]{0:T(128)} %segments.1, bf16[256,8192]{1,0:T(8,128)(2,1)} %tok.1, bf16[8192,512]{1,0:T(8,128)(2,1)} %weight.1, bf16[16,256,128]{2,1,0:T(8,128)(2,1)} %down.1, bf16[128,512]{1,0:T(8,128)(2,1)} %bitcast.3), custom_call_target="tpu_custom_call" | custom-call | tf_op jit(solution)/shard_map/pallas_call | solution.py:499
  102.1 2.3 %copy.8 = bf16[1024,512]{1,0:T(8,128)(2,1)} copy(bf16[1024,512]{1,0:T(8,128)(2,1)} %bitcast.2) | data formatting | bytes 2097152

commit v4 on v3

--- a/solution.py
+++ b/solution.py
@@ -9,6 +9,7 @@
 
 MESH = pl.DeviceIdType.MESH
 AHEAD = 6
+PARTS = 4
 
 
 def plain(
@@ -60,13 +61,15 @@
 def kernel(
     n_dp,
     up_rank,
-    requests,
-    segments,
+    requests_in,
+    segments_in,
     tok,
     weight,
     down,
     up,
     out,
+    requests,
+    segments,
     t_all,
     w_all,
     d_own,
@@ -205,6 +208,11 @@
         return at_place(place + (k + 1) // 2 * (1 - 2 * (k % 2)))
 
     def columns(i, side):
+        part_of = i - (pieces - 1)
+        if isinstance(i, int) and part_of >= 0:
+            width = piece // PARTS
+            start = near(n_dp - 1) * (4 * tile) + ((side + 1) % 2) * piece + part_of * width
+            return pl.ds(pl.multiple_of(start, width), width)
         start = near(i % n_dp) * (4 * tile) + ((side + i // n_dp) % 2) * piece
         return pl.ds(pl.multiple_of(start, piece), piece)
 
@@ -246,6 +254,10 @@
     u_local = pltpu.make_async_copy(
         up, u_all.at[pl.ds(pl.multiple_of(group * up_rows, up_rows), up_rows)], local_sem.at[3]
     )
+    r_local = pltpu.make_async_copy(requests_in, requests, local_sem.at[4])
+    s_local = pltpu.make_async_copy(segments_in, segments, local_sem.at[5])
+    r_local.start()
+    s_local.start()
     t_local.start()
     w_local.start()
     d_local.start()
@@ -318,6 +330,8 @@
 
     d_local.wait()
     u_local.wait()
+    r_local.wait()
+    s_local.wait()
 
     @pl.loop(0, 4)
     def _(k):
@@ -395,7 +409,8 @@
     swap_out[1] = jnp.where(y == 0, key_part, value_part)
     hop2 = remote(swap_out.at[0], swap_in, hop_send.at[1], hop_recv.at[1], (group, across))
     hop2.start()
-    y_copy(pieces - 1).start()
+    for i in range(pieces - 1, pieces - 1 + PARTS):
+        y_copy(i).start()
 
     take_piece(11)
     for way in range(2):
@@ -444,21 +459,11 @@
 
     out[me] = acc[me].astype(jnp.bfloat16)
     out[sibling] = acc[sibling].astype(jnp.bfloat16)
-    take_piece(pieces - 1)
-    out[across] = acc[across].astype(jnp.bfloat16)
-    fwd_arrival(pieces - 1).wait_recv()
-    add(diagonal, columns(pieces - 1, y))
-    out[diagonal] = acc[diagonal].astype(jnp.bfloat16)
 
     pair.wait_send()
     hop1.wait_send()
     hop2.wait_send()
     hop3.wait_send()
-
-    @pl.loop(0, pieces)
-    def _(i):
-        fwd_copy(i).wait_send()
-
     for way in range(2):
         for k in range(4):
             one(way, k).wait_send()
@@ -468,6 +473,29 @@
         four_picked(way).wait_send()
         for step in range(4):
             u_copy(way, step).wait_send()
+
+    @pl.loop(0, pieces - 2)
+    def _(i):
+        fwd_copy(i).wait_send()
+
+    fwd_arrival(pieces - 2).wait_recv()
+    add(diagonal, columns(pieces - 2, y))
+
+    tail = range(pieces - 1, pieces - 1 + PARTS)
+    for i in tail:
+        y_arrival(i).wait_recv()
+        fwd_copy(i).start()
+    whole = pl.ds(pl.multiple_of(near(n_dp - 1) * (4 * tile) + other_y * piece, piece), piece)
+    add(across, whole)
+    out[across] = acc[across].astype(jnp.bfloat16)
+    for i in tail:
+        fwd_arrival(i).wait_recv()
+    add(diagonal, whole)
+    out[diagonal] = acc[diagonal].astype(jnp.bfloat16)
+    for i in tail:
+        y_copy(i).wait_send()
+    for i in range(pieces - 2, pieces - 1 + PARTS):
+        fwd_copy(i).wait_send()
 
 
 def on_device(
@@ -499,10 +527,11 @@
     result = pl.pallas_call(
         functools.partial(kernel, n_dp, up_rank),
         out_shape=jax.ShapeDtypeStruct((n_mp, rows, width), bf16),
-        in_specs=[pl.BlockSpec(memory_space=pltpu.SMEM)] * 2
-        + [pl.BlockSpec(memory_space=pl.ANY)] * 4,
+        in_specs=[pl.BlockSpec(memory_space=pltpu.HBM)] * 6,
         out_specs=vmem,
         scratch_shapes=[
+            pltpu.SMEM(adapter_per_request.shape, jnp.int32),
+            pltpu.SMEM(request_per_segment.shape, jnp.int32),
             pltpu.VMEM((n_mp, rows, depth), bf16),
             pltpu.VMEM((depth, width), bf16),
             pltpu.VMEM((adapters, tile, double_rank), bf16),
@@ -521,13 +550,13 @@
             pltpu.VMEM((rows, double_rank), f32),
             pltpu.VMEM((2, rows, double_rank), bf16),
             pltpu.VMEM((seg_group, double_rank, width), bf16),
-            dma((4,)),
+            dma((6,)),
             dma,
             dma,
-            dma((2 * n_dp,)),
-            dma((2 * n_dp,)),
-            dma((2 * n_dp,)),
-            dma((2 * n_dp,)),
+            dma((2 * n_dp + PARTS - 1,)),
+            dma((2 * n_dp + PARTS - 1,)),
+            dma((2 * n_dp + PARTS - 1,)),
+            dma((2 * n_dp + PARTS - 1,)),
             dma((2, 14)),
             dma((2, 14)),
             dma((2, 4)),
@@ -536,11 +565,16 @@
             dma((3,)),
         ],
         compiler_params=pltpu.CompilerParams(
-            collective_id=0, has_side_effects=True, vmem_limit_bytes=63 * 2**20
+            collective_id=0, has_side_effects=True, vmem_limit_bytes=52 * 2**20
         ),
     )(
-        adapter_per_request, request_per_segment, tokens, key_value_weight, adapter_down_weight,
-        adapter_up_weight.reshape(up_rows, width),
+        *(
+            pltpu.with_memory_space_constraint(a, pltpu.HBM)
+            for a in (
+                adapter_per_request, request_per_segment, tokens, key_value_weight,
+                adapter_down_weight, adapter_up_weight.reshape(up_rows, width),
+            )
+        )
     )
     return result.reshape(n_mp * rows, width)
 

time: 105 us -> 102 us (0.971)
  Pallas kernels: 102 us -> 100 us
  local copies, waits for them, and re-layouts: 2.26 us -> 0.97 us
    pallas_call x1, Pallas kernels: 102 us -> 100 us  [on_device(): pl.pallas_call(functools.partial(kernel, n_dp, up_rank), out_shape=jax.Sh...]
    unnamed x1, local copies, waits for them, and re-layouts: 2.26 us -> 0.97 us
where the time goes in v4:
time: 102 us; the launch traced here: 101 us
  Pallas kernels  100 us (98%)
    pallas_call x1, Pallas kernels, on_device(): pl.pallas_call(functools.partial(kernel, n_dp, up_rank), out_shape=jax.Sh...  100 us

profile of v4, /device:TPU:0, one launch (start us, length us, event | category | flops | bytes accessed | tf_op | source)
XLA Modules:
  0.0 101.2 jit_solution(15744753612016739564)
XLA Ops:
  0.0 100.2 %shard_map.64 = bf16[4,256,512]{2,1,0:T(8,128)(2,1)S(1)} custom-call(s32[32]{0:T(128)} %requests_in.1, s32[64]{0:T(128)} %segments_in.1, bf16[256,8192]{1,0:T(8,128)(2,1)} %tok.1, bf16[8192,512]{1,0:T(8,128)(2,1)} %weight.1, bf16[16,256,128]{2,1,0:T(8,128)(2,1)} %down.1, bf16[128,512]{1,0:T(8,128)(2,1)} %bitcast.3), custom_call_target="tpu_custom_call" | custom-call | tf_op jit(solution)/shard_map/pallas_call | solution.py:527
  100.2 1.0 copy.8

commit v5 on v4

--- a/solution.py
+++ b/solution.py
@@ -84,6 +84,7 @@
     acc,
     part,
     part_in,
+    kept,
     swap_out,
     swap_in,
     low,
@@ -248,6 +249,8 @@
     for k in range(4):
         for way in range(2):
             one(way, k).start()
+    for way in range(2):
+        u_copy(way, 0).start()
     t_local = pltpu.make_async_copy(tok, t_all.at[me], local_sem.at[0])
     w_local = pltpu.make_async_copy(weight, w_all, local_sem.at[1])
     d_local = pltpu.make_async_copy(down, d_own, local_sem.at[2])
@@ -328,6 +331,9 @@
         def _():
             take_piece(k - 1)
 
+    for way in range(2):
+        u_arrival(way, 0).wait_recv()
+        u_copy(way, 1).start()
     d_local.wait()
     u_local.wait()
     r_local.wait()
@@ -376,8 +382,11 @@
     for way in range(2):
         four_picked(way).start()
     for way in range(2):
-        u_copy(way, 0).start()
+        u_arrival(way, 1).wait_recv()
+        u_copy(way, 2).start()
     take_piece(9)
+    for i in range(pieces - 1, pieces - 1 + PARTS // 2):
+        y_copy(i).start()
     for way in range(2):
         three_picked(way).wait_recv()
     add_low(
@@ -397,30 +406,23 @@
 
     hop1 = remote(part.at[1 - core], part_in, hop_send.at[0], hop_recv.at[0], (group, sibling))
     hop1.start()
-    for way in range(2):
-        u_arrival(way, 0).wait_recv()
-        u_copy(way, 1).start()
     hop1.wait_recv()
     q0 = part[core, 0] + part_in[0]
     q1 = part[core, 1] + part_in[1]
     key_part = jnp.concatenate([q0[:, :rank], q1[:, :rank]], axis=1)
     value_part = jnp.concatenate([q0[:, rank:], q1[:, rank:]], axis=1)
-    swap_out[0] = jnp.where(y == 0, value_part, key_part)
-    swap_out[1] = jnp.where(y == 0, key_part, value_part)
-    hop2 = remote(swap_out.at[0], swap_in, hop_send.at[1], hop_recv.at[1], (group, across))
+    swap_out[...] = jnp.where(y == 0, value_part, key_part).astype(jnp.bfloat16)
+    kept[...] = jnp.where(y == 0, key_part, value_part)
+    hop2 = remote(swap_out, swap_in, hop_send.at[1], hop_recv.at[1], (group, across))
     hop2.start()
-    for i in range(pieces - 1, pieces - 1 + PARTS):
+    for i in range(pieces - 1 + PARTS // 2, pieces - 1 + PARTS):
         y_copy(i).start()
-
-    take_piece(11)
-    for way in range(2):
-        u_arrival(way, 1).wait_recv()
-        u_copy(way, 2).start()
-    take_piece(12)
     for way in range(2):
         u_arrival(way, 2).wait_recv()
         u_copy(way, 3).start()
-    take_piece(13)
+
+    take_piece(11)
+    take_piece(12)
     for way in range(2):
         u_arrival(way, 3).wait_recv()
 
@@ -440,8 +442,9 @@
             jnp.bfloat16
         )
 
+    take_piece(13)
     hop2.wait_recv()
-    low[core] = (swap_out[1] + swap_in[...]).astype(jnp.bfloat16)
+    low[core] = (kept[...] + swap_in[...].astype(jnp.float32)).astype(jnp.bfloat16)
     hop3 = remote(low.at[core], low.at[core], hop_send.at[2], hop_recv.at[2], (group, sibling))
     hop3.start()
     take_piece(pieces - 2)
@@ -482,15 +485,23 @@
     add(diagonal, columns(pieces - 2, y))
 
     tail = range(pieces - 1, pieces - 1 + PARTS)
-    for i in tail:
+    final = pieces - 2 + PARTS
+    start = near(n_dp - 1) * (4 * tile) + other_y * piece
+    width = piece // PARTS
+    early = pl.ds(pl.multiple_of(start, width), piece - width)
+    for i in tail[:-1]:
         y_arrival(i).wait_recv()
         fwd_copy(i).start()
-    whole = pl.ds(pl.multiple_of(near(n_dp - 1) * (4 * tile) + other_y * piece, piece), piece)
-    add(across, whole)
+    add(across, early)
+    for i in tail[:-1]:
+        fwd_arrival(i).wait_recv()
+    add(diagonal, early)
+    y_arrival(final).wait_recv()
+    fwd_copy(final).start()
+    add(across, columns(final, y))
     out[across] = acc[across].astype(jnp.bfloat16)
-    for i in tail:
-        fwd_arrival(i).wait_recv()
-    add(diagonal, whole)
+    fwd_arrival(final).wait_recv()
+    add(diagonal, columns(final, y))
     out[diagonal] = acc[diagonal].astype(jnp.bfloat16)
     for i in tail:
         y_copy(i).wait_send()
@@ -546,8 +557,9 @@
             pltpu.VMEM((n_mp, rows, width), f32),
             pltpu.VMEM((2, 2, rows, double_rank), f32),
             pltpu.VMEM((2, rows, double_rank), f32),
-            pltpu.VMEM((2, rows, double_rank), f32),
             pltpu.VMEM((rows, double_rank), f32),
+            pltpu.VMEM((rows, double_rank), bf16),
+            pltpu.VMEM((rows, double_rank), bf16),
             pltpu.VMEM((2, rows, double_rank), bf16),
             pltpu.VMEM((seg_group, double_rank, width), bf16),
             dma((6,)),

time: 102 us -> 103 us (level)
  Pallas kernels: 100 us -> 102 us
    pallas_call x1, Pallas kernels: 100 us -> 102 us  [on_device(): pl.pallas_call(functools.partial(kernel, n_dp, up_rank), out_shape=jax.Sh...]
where the time goes in v5:
time: 103 us
  Pallas kernels  102 us (99%)
    pallas_call x1, Pallas kernels, on_device(): pl.pallas_call(functools.partial(kernel, n_dp, up_rank), out_shape=jax.Sh...  102 us

profile of v5, /device:TPU:0, one launch (start us, length us, event | category | flops | bytes accessed | tf_op | source)
XLA Modules:
  0.0 102.5 jit_solution(12465106628454692994)
XLA Ops:
  0.0 101.5 %shard_map.64 = bf16[4,256,512]{2,1,0:T(8,128)(2,1)S(1)} custom-call(s32[32]{0:T(128)} %requests_in.1, s32[64]{0:T(128)} %segments_in.1, bf16[256,8192]{1,0:T(8,128)(2,1)} %tok.1, bf16[8192,512]{1,0:T(8,128)(2,1)} %weight.1, bf16[16,256,128]{2,1,0:T(8,128)(2,1)} %down.1, bf16[128,512]{1,0:T(8,128)(2,1)} %bitcast.3), custom_call_target="tpu_custom_call" | custom-call | tf_op jit(solution)/shard_map/pallas_call | solution.py:538
  101.5 1.0 copy.8

commit v6 on v4

--- a/solution.py
+++ b/solution.py
@@ -283,7 +283,7 @@
         fwd_copy(i).start()
         y_copy(i).wait_send()
 
-        @pl.when(i + AHEAD < pieces - 1)
+        @pl.when(i + AHEAD < pieces - 2)
         def _():
             y_copy(i + AHEAD).start()
 
@@ -397,9 +397,6 @@
 
     hop1 = remote(part.at[1 - core], part_in, hop_send.at[0], hop_recv.at[0], (group, sibling))
     hop1.start()
-    for way in range(2):
-        u_arrival(way, 0).wait_recv()
-        u_copy(way, 1).start()
     hop1.wait_recv()
     q0 = part[core, 0] + part_in[0]
     q1 = part[core, 1] + part_in[1]
@@ -409,8 +406,11 @@
     swap_out[1] = jnp.where(y == 0, key_part, value_part)
     hop2 = remote(swap_out.at[0], swap_in, hop_send.at[1], hop_recv.at[1], (group, across))
     hop2.start()
-    for i in range(pieces - 1, pieces - 1 + PARTS):
+    for i in range(pieces - 2, pieces - 1 + PARTS):
         y_copy(i).start()
+    for way in range(2):
+        u_arrival(way, 0).wait_recv()
+        u_copy(way, 1).start()
 
     take_piece(11)
     for way in range(2):
@@ -421,6 +421,10 @@
         u_arrival(way, 2).wait_recv()
         u_copy(way, 3).start()
     take_piece(13)
+    hop2.wait_recv()
+    low[core] = (swap_out[1] + swap_in[...]).astype(jnp.bfloat16)
+    hop3 = remote(low.at[core], low.at[core], hop_send.at[2], hop_recv.at[2], (group, sibling))
+    hop3.start()
     for way in range(2):
         u_arrival(way, 3).wait_recv()
 
@@ -440,11 +444,6 @@
             jnp.bfloat16
         )
 
-    hop2.wait_recv()
-    low[core] = (swap_out[1] + swap_in[...]).astype(jnp.bfloat16)
-    hop3 = remote(low.at[core], low.at[core], hop_send.at[2], hop_recv.at[2], (group, sibling))
-    hop3.start()
-    take_piece(pieces - 2)
     remote(
         low.at[1 - core], low.at[1 - core], hop_send.at[2], hop_recv.at[2], (group, sibling)
     ).wait_recv()
@@ -460,6 +459,7 @@
     out[me] = acc[me].astype(jnp.bfloat16)
     out[sibling] = acc[sibling].astype(jnp.bfloat16)
 
+    take_piece(pieces - 2)
     pair.wait_send()
     hop1.wait_send()
     hop2.wait_send()
@@ -482,15 +482,23 @@
     add(diagonal, columns(pieces - 2, y))
 
     tail = range(pieces - 1, pieces - 1 + PARTS)
-    for i in tail:
+    final = pieces - 2 + PARTS
+    start = near(n_dp - 1) * (4 * tile) + other_y * piece
+    width = piece // PARTS
+    early = pl.ds(pl.multiple_of(start, width), piece - width)
+    for i in tail[:-1]:
         y_arrival(i).wait_recv()
         fwd_copy(i).start()
-    whole = pl.ds(pl.multiple_of(near(n_dp - 1) * (4 * tile) + other_y * piece, piece), piece)
-    add(across, whole)
+    add(across, early)
+    for i in tail[:-1]:
+        fwd_arrival(i).wait_recv()
+    add(diagonal, early)
+    y_arrival(final).wait_recv()
+    fwd_copy(final).start()
+    add(across, columns(final, y))
     out[across] = acc[across].astype(jnp.bfloat16)
-    for i in tail:
-        fwd_arrival(i).wait_recv()
-    add(diagonal, whole)
+    fwd_arrival(final).wait_recv()
+    add(diagonal, columns(final, y))
     out[diagonal] = acc[diagonal].astype(jnp.bfloat16)
     for i in tail:
         y_copy(i).wait_send()

time: 102 us -> 102 us (level)
  no operation moved by 1% of the time
where the time goes in v6:
time: 102 us
  Pallas kernels  101 us (99%)
    pallas_call x1, Pallas kernels, on_device(): pl.pallas_call(functools.partial(kernel, n_dp, up_rank), out_shape=jax.Sh...  101 us

profile of v6, /device:TPU:0, one launch (start us, length us, event | category | flops | bytes accessed | tf_op | source)
XLA Modules:
  0.0 102.1 jit_solution(9419984268143142837)
XLA Ops:
  0.0 101.1 %shard_map.64 = bf16[4,256,512]{2,1,0:T(8,128)(2,1)S(1)} custom-call(s32[32]{0:T(128)} %requests_in.1, s32[64]{0:T(128)} %segments_in.1, bf16[256,8192]{1,0:T(8,128)(2,1)} %tok.1, bf16[8192,512]{1,0:T(8,128)(2,1)} %weight.1, bf16[16,256,128]{2,1,0:T(8,128)(2,1)} %down.1, bf16[128,512]{1,0:T(8,128)(2,1)} %bitcast.3), custom_call_target="tpu_custom_call" | custom-call | tf_op jit(solution)/shard_map/pallas_call | solution.py:535
  101.1 1.0 copy.8

commit v7 on v6

--- a/solution.py
+++ b/solution.py
@@ -283,7 +283,7 @@
         fwd_copy(i).start()
         y_copy(i).wait_send()
 
-        @pl.when(i + AHEAD < pieces - 2)
+        @pl.when(i + AHEAD < pieces - 1)
         def _():
             y_copy(i + AHEAD).start()
 
@@ -406,7 +406,7 @@
     swap_out[1] = jnp.where(y == 0, key_part, value_part)
     hop2 = remote(swap_out.at[0], swap_in, hop_send.at[1], hop_recv.at[1], (group, across))
     hop2.start()
-    for i in range(pieces - 2, pieces - 1 + PARTS):
+    for i in range(pieces - 1, pieces - 1 + PARTS):
         y_copy(i).start()
     for way in range(2):
         u_arrival(way, 0).wait_recv()
@@ -421,10 +421,6 @@
         u_arrival(way, 2).wait_recv()
         u_copy(way, 3).start()
     take_piece(13)
-    hop2.wait_recv()
-    low[core] = (swap_out[1] + swap_in[...]).astype(jnp.bfloat16)
-    hop3 = remote(low.at[core], low.at[core], hop_send.at[2], hop_recv.at[2], (group, sibling))
-    hop3.start()
     for way in range(2):
         u_arrival(way, 3).wait_recv()
 
@@ -444,6 +440,11 @@
             jnp.bfloat16
         )
 
+    hop2.wait_recv()
+    low[core] = (swap_out[1] + swap_in[...]).astype(jnp.bfloat16)
+    hop3 = remote(low.at[core], low.at[core], hop_send.at[2], hop_recv.at[2], (group, sibling))
+    hop3.start()
+    take_piece(pieces - 2)
     remote(
         low.at[1 - core], low.at[1 - core], hop_send.at[2], hop_recv.at[2], (group, sibling)
     ).wait_recv()
@@ -459,7 +460,6 @@
     out[me] = acc[me].astype(jnp.bfloat16)
     out[sibling] = acc[sibling].astype(jnp.bfloat16)
 
-    take_piece(pieces - 2)
     pair.wait_send()
     hop1.wait_send()
     hop2.wait_send()

time: 102 us -> 102 us (level)
  no operation moved by 1% of the time
where the time goes in v7:
time: 102 us
  Pallas kernels  101 us (99%)
    pallas_call x1, Pallas kernels, on_device(): pl.pallas_call(functools.partial(kernel, n_dp, up_rank), out_shape=jax.Sh...  101 us

profile of v7, /device:TPU:0, one launch (start us, length us, event | category | flops | bytes accessed | tf_op | source)
XLA Modules:
  0.0 102.1 jit_solution(8215450643270395804)
XLA Ops:
  0.0 101.1 %shard_map.64 = bf16[4,256,512]{2,1,0:T(8,128)(2,1)S(1)} custom-call(s32[32]{0:T(128)} %requests_in.1, s32[64]{0:T(128)} %segments_in.1, bf16[256,8192]{1,0:T(8,128)(2,1)} %tok.1, bf16[8192,512]{1,0:T(8,128)(2,1)} %weight.1, bf16[16,256,128]{2,1,0:T(8,128)(2,1)} %down.1, bf16[128,512]{1,0:T(8,128)(2,1)} %bitcast.3), custom_call_target="tpu_custom_call" | custom-call | tf_op jit(solution)/shard_map/pallas_call | solution.py:535
  101.1 1.0 copy.8
